TPU v7x, 256 devices: a whole 4x4x8 slice. The times are simulated.
256 devices in a mesh: grp: 16 (over y, x), sp: 8 (over z), tp: 2 (over core).
Axes of the slice: x: 4, y: 4, z: 8, core: 2. Of those that a mesh axis runs over, the one named last changes fastest.
Arguments:
- q_spatial: bfloat16 [32768, 3072], P(('grp', 'sp'), 'tp'), may hold values from -130 to 130
- k_spatial: bfloat16 [32768, 3072], P(('grp', 'sp'), 'tp'), may hold values from -5 to 5
- v_spatial: bfloat16 [32768, 3072], P(('grp', 'sp'), 'tp'), may hold values from -6 to 6
- q_temporal: bfloat16 [32768, 3072], P(('grp', 'sp'), 'tp'), may hold values from -130 to 130
- k_temporal: bfloat16 [32768, 3072], P(('grp', 'sp'), 'tp'), may hold values from -5 to 5
- out_weight: bfloat16 [3072, 3072], P('tp', ('grp', 'sp')), may hold values from -0.109375 to 0.109375
- frame_video: int32 [256], replicated, may hold values from 0 to 15, never falling along the last dimension, each value on 1 to 32 neighbouring positions
- video_patches: int32 [16], replicated, may hold values from 64 to 128, as said below
Outputs:
- mixed: bfloat16 [32768, 3072], P(('grp', 'sp'), 'tp')
Inputs may be any that keep to these rules, and one draw needn't show every extreme that they name: `video_patches`: between 64 and 128; some video has exactly 128.
All inputs are finite; a program needn't handle non-finite values.
Results may differ from a plain program's by a relative error of at most 0.014.
Values may be sent and summed in bfloat16 or wider, within the bound.
A program may use at most 128 MiB of HBM per device.

v0:
```python
import jax
import jax.numpy as jnp
from jax import lax
from jax.sharding import PartitionSpec as P

HD = 128
PMAX = 128


def soft_weights(scores, mask):
    masked = jnp.where(mask, scores, jnp.float32(-1e30))
    top = jnp.max(masked, axis=-1, keepdims=True)
    expo = jnp.where(mask, jnp.exp(scores - top), jnp.float32(0.0))
    return (expo / jnp.sum(expo, axis=-1, keepdims=True)).astype(jnp.bfloat16)


def per_device(
    q_spatial, k_spatial, v_spatial, q_temporal, k_temporal, out_weight, frame_video, video_patches
):
    rows, feats = q_spatial.shape
    heads = feats // HD
    scale = HD ** (-0.5)
    frames_dev = rows // PMAX
    groups = lax.axis_size(("grp", "sp"))
    patch_dev = PMAX // groups
    all_frames = frame_video.shape[0]
    first = lax.axis_index(("grp", "sp")) * frames_dev
    my_video = lax.dynamic_slice_in_dim(frame_video, first, frames_dev)
    match = my_video[:, None] == jnp.arange(video_patches.shape[0], dtype=jnp.int32)[None, :]
    my_patches = jnp.sum(jnp.where(match, video_patches[None, :], 0), axis=1)
    live = jnp.arange(PMAX, dtype=jnp.int32)[None, :] < my_patches[:, None]
    shape4 = (frames_dev, PMAX, heads, HD)
    scores = (
        jnp.einsum(
            "fphd,fkhd->fhpk",
            q_spatial.reshape(shape4),
            k_spatial.reshape(shape4),
            preferred_element_type=jnp.float32,
        )
        * scale
    )
    weights = soft_weights(scores, live[:, None, None, :])
    spatial = jnp.einsum(
        "fhpk,fkhd->fphd", weights, v_spatial.reshape(shape4), preferred_element_type=jnp.float32
    ).astype(jnp.bfloat16)
    spatial = spatial.reshape(frames_dev, PMAX, feats)
    q_frames = q_temporal.reshape(frames_dev, PMAX, feats)
    k_frames = k_temporal.reshape(frames_dev, PMAX, feats)
    wide = (1, frames_dev, groups, patch_dev, feats)
    q_patch, k_patch, v_patch = (
        lax.all_to_all(
            q_frames.reshape(wide), ("grp", "sp"), split_axis=2, concat_axis=0, tiled=True
        ),
        lax.all_to_all(
            k_frames.reshape(wide), ("grp", "sp"), split_axis=2, concat_axis=0, tiled=True
        ),
        lax.all_to_all(
            spatial.reshape(wide), ("grp", "sp"), split_axis=2, concat_axis=0, tiled=True
        ),
    )
    tshape = (all_frames, patch_dev, heads, HD)
    same = frame_video[:, None] == frame_video[None, :]
    tscores = (
        jnp.einsum(
            "fbhd,gbhd->bhfg",
            q_patch.reshape(tshape),
            k_patch.reshape(tshape),
            preferred_element_type=jnp.float32,
        )
        * scale
    )
    tweights = soft_weights(tscores, same[None, None, :, :])
    temporal = jnp.einsum(
        "bhfg,gbhd->fbhd", tweights, v_patch.reshape(tshape), preferred_element_type=jnp.float32
    ).astype(jnp.bfloat16)
    back = lax.all_to_all(
        temporal.reshape(groups, frames_dev, 1, patch_dev, feats),
        ("grp", "sp"),
        split_axis=0,
        concat_axis=2,
        tiled=True,
    )
    tmix = back.reshape(rows, feats)
    partial_rows = jnp.dot(
        tmix,
        lax.all_gather(out_weight, ("grp", "sp"), axis=1, tiled=True),
        preferred_element_type=jnp.float32,
    )
    summed = lax.psum_scatter(partial_rows, "tp", scatter_dimension=1, tiled=True)
    alive = live.reshape(rows)
    return jnp.where(alive[:, None], summed, jnp.float32(0.0)).astype(jnp.bfloat16)


def solution(mesh):
    return jax.shard_map(
        per_device,
        mesh=mesh,
        in_specs=(
            P(("grp", "sp"), "tp"),
            P(("grp", "sp"), "tp"),
            P(("grp", "sp"), "tp"),
            P(("grp", "sp"), "tp"),
            P(("grp", "sp"), "tp"),
            P("tp", ("grp", "sp")),
            P(),
            P(),
        ),
        out_specs=P(("grp", "sp"), "tp"),
        check_vma=False,
    )
```

profile of v0, /device:TPU:1, one launch (start us, length us, event | category | flops | bytes accessed | tf_op | source)
XLA Modules:
  0.0 199.3 jit_solution(959483004015348147)
XLA Ops:
  6.5 0.7 all-gather.2.cloned.1.call-update
  7.3 1.6 reshape.127
  8.9 1.6 reshape.128
  10.5 1.6 reshape.129
  12.5 0.7 convolution_multiply_fusion
  13.2 0.6 fusion.31
  14.3 1.8 copy.70
  16.1 16.3 %all-to-all-start = ((bf16[1,2,128,1,1536]{4,1,3,0,2:T(2,128)(2,1)}), bf16[1,2,128,1,1536]{4,1,3,0,2:T(2,128)(2,1)S(1)}, u32[]{:S(2)}, u32[]{:S(2)}) async-start(bf16[1,2,128,1,1536]{4,1,3,0,2:T(2,128)(2,1)} %copy.70), calls=%async_computation | async-start | bytes 1572864 | tf_op jit(solution)/shard_map/all_to_all | solution.py:57
  32.5 1.7 copy.71
  34.2 24.6 %all-to-all-done = bf16[1,2,128,1,1536]{4,1,3,0,2:T(2,128)(2,1)S(1)} async-done(((bf16[1,2,128,1,1536]{4,1,3,0,2:T(2,128)(2,1)}), bf16[1,2,128,1,1536]{4,1,3,0,2:T(2,128)(2,1)S(1)}, u32[]{:S(2)}, u32[]{:S(2)}) %all-to-all-start) | async-done | bytes 786464 | tf_op jit(solution)/shard_map/all_to_all | solution.py:57
  58.8 6.2 %all-to-all-start.1 = ((bf16[1,2,128,1,1536]{4,1,3,0,2:T(2,128)(2,1)}), bf16[1,2,128,1,1536]{4,1,3,0,2:T(2,128)(2,1)S(1)}, u32[]{:S(2)}, u32[]{:S(2)}) async-start(bf16[1,2,128,1,1536]{4,1,3,0,2:T(2,128)(2,1)} %copy.71), calls=%async_computation.1 | async-start | bytes 1572864 | tf_op jit(solution)/shard_map/all_to_all | solution.py:51
  65.0 1.7 copy.72
  66.7 26.1 %all-to-all-done.1 = bf16[1,2,128,1,1536]{4,1,3,0,2:T(2,128)(2,1)S(1)} async-done(((bf16[1,2,128,1,1536]{4,1,3,0,2:T(2,128)(2,1)}), bf16[1,2,128,1,1536]{4,1,3,0,2:T(2,128)(2,1)S(1)}, u32[]{:S(2)}, u32[]{:S(2)}) %all-to-all-start.1) | async-done | bytes 786464 | tf_op jit(solution)/shard_map/all_to_all | solution.py:51
  92.8 6.8 %all-to-all-start.2 = ((bf16[1,2,128,1,1536]{4,1,3,0,2:T(2,128)(2,1)}), bf16[1,2,128,1,1536]{4,1,3,0,2:T(2,128)(2,1)S(1)}, u32[]{:S(2)}, u32[]{:S(2)}) async-start(bf16[1,2,128,1,1536]{4,1,3,0,2:T(2,128)(2,1)} %copy.72), calls=%async_computation.2 | async-start | bytes 1572864 | tf_op jit(solution)/shard_map/all_to_all | solution.py:54
  99.9 1.5 reshape.122
  101.9 19.8 %all-to-all-done.2 = bf16[1,2,128,1,1536]{4,1,3,0,2:T(2,128)(2,1)S(1)} async-done(((bf16[1,2,128,1,1536]{4,1,3,0,2:T(2,128)(2,1)}), bf16[1,2,128,1,1536]{4,1,3,0,2:T(2,128)(2,1)S(1)}, u32[]{:S(2)}, u32[]{:S(2)}) %all-to-all-start.2) | async-done | bytes 786464 | tf_op jit(solution)/shard_map/all_to_all | solution.py:54
  122.2 0.6 fusion.19
  122.8 1.3 fusion.30
  124.7 1.0 copy.77
  126.1 35.6 %all_to_all.60 = bf16[128,2,1,1,1536]{4,1,3,2,0:T(2,128)(2,1)S(1)} all-to-all(bf16[128,2,1,1,1536]{4,1,3,2,0:T(2,128)(2,1)S(1)} %bitcast.39), channel_id=1, replica_groups=mesh['grp'=16,'sp'=8,'tp'=2] {'grp','sp'}, dimensions={0} | all-to-all | bytes 1572864 | tf_op jit(solution)/shard_map/all_to_all | solution.py:76
  161.8 3.6 %all-gather.2.cloned.1.call-done = bf16[1536,3072]{0,1:T(8,128)(2,1)} async-done(((bf16[1536,24]{0,1:T(8,128)(2,1)}), bf16[1536,3072]{0,1:T(8,128)(2,1)}) %all-gather.2.cloned.1.call-update) | async-done | bytes 9437200 | tf_op jit(solution)/shard_map/all_gather | solution.py:86
  165.4 8.0 %fusion.32 = f32[256,3072]{1,0:T(8,128)} fusion(bf16[256,1536]{1,0:T(8,128)(2,1)S(1)} %bitcast.42, bf16[1536,3072]{0,1:T(8,128)(2,1)} %all-gather.2.cloned.1.call-done), kind=kOutput, calls=%fused_computation.40 | convolution fusion | flops 2415919104 | bytes 13369344 | tf_op jit(solution)/shard_map/dot_general | solution.py:84
  173.4 16.7 %reduce-scatter.2.cloned.1.call-done = f32[256,1536]{1,0:T(8,128)} async-done(((f32[256,3072]{1,0:T(8,128)}), f32[256,1536]{1,0:T(8,128)}) %reduce-scatter.2.cloned.1.call-update) | async-done | bytes 1572880 | tf_op jit(solution)/shard_map/reduce_scatter | solution.py:89
  190.0 2.4 %select_convert_fusion = bf16[256,1536]{1,0:T(8,128)(2,1)} fusion(f32[256,1536]{1,0:T(8,128)} %reduce-scatter.2.cloned.1.call-done, pred[256]{0:T(512)(128)(4,1)S(1)} %get-tuple-element.5), kind=kLoop, calls=%fused_computation.7 | loop fusion | flops 393216 | bytes 2359552 | tf_op jit(solution)/shard_map/convert_element_type | solution.py:91
  (23 shorter events, 3.2 us)
Async XLA Ops:
  6.5 5.7 %copy-start.3 = (s32[256]{0:T(256)S(1)}, s32[256]{0:T(256)}, u32[]{:S(2)}) copy-start(s32[256]{0:T(256)} %param.14) | copy-start | bytes 3076
  6.5 5.7 %copy-start.4 = (s32[16]{0:T(128)S(1)}, s32[16]{0:T(128)}, u32[]{:S(2)}) copy-start(s32[16]{0:T(128)} %param.15) | copy-start | bytes 196
  6.5 158.8 %all-gather.2.cloned.1.call-start = ((), (), s32[]{:S(2)}) async-start(), calls=%async_computation.5 | async-start | bytes 9510912 | tf_op jit(solution)/shard_map/all_gather | solution.py:86
  14.3 18.2 %copy-start.1 = (bf16[256,1536]{1,0:T(8,128)(2,1)S(1)}, bf16[256,1536]{1,0:T(8,128)(2,1)}, u32[]{:S(2)}) copy-start(bf16[256,1536]{1,0:T(8,128)(2,1)} %param.11) | copy-start | bytes 2359300
  14.3 50.7 %copy-start.2 = (bf16[256,1536]{1,0:T(8,128)(2,1)S(1)}, bf16[256,1536]{1,0:T(8,128)(2,1)}, u32[]{:S(2)}) copy-start(bf16[256,1536]{1,0:T(8,128)(2,1)} %param.12) | copy-start | bytes 2359300
  16.1 42.7 %all-to-all-start = ((bf16[1,2,128,1,1536]{4,1,3,0,2:T(2,128)(2,1)}), bf16[1,2,128,1,1536]{4,1,3,0,2:T(2,128)(2,1)S(1)}, u32[]{:S(2)}, u32[]{:S(2)}) async-start(bf16[1,2,128,1,1536]{4,1,3,0,2:T(2,128)(2,1)} %copy.70), calls=%async_computation | async-start | bytes 1572864 | tf_op jit(solution)/shard_map/all_to_all | solution.py:57
  58.8 34.0 %all-to-all-start.1 = ((bf16[1,2,128,1,1536]{4,1,3,0,2:T(2,128)(2,1)}), bf16[1,2,128,1,1536]{4,1,3,0,2:T(2,128)(2,1)S(1)}, u32[]{:S(2)}, u32[]{:S(2)}) async-start(bf16[1,2,128,1,1536]{4,1,3,0,2:T(2,128)(2,1)} %copy.71), calls=%async_computation.1 | async-start | bytes 1572864 | tf_op jit(solution)/shard_map/all_to_all | solution.py:51
  92.8 28.9 %all-to-all-start.2 = ((bf16[1,2,128,1,1536]{4,1,3,0,2:T(2,128)(2,1)}), bf16[1,2,128,1,1536]{4,1,3,0,2:T(2,128)(2,1)S(1)}, u32[]{:S(2)}, u32[]{:S(2)}) async-start(bf16[1,2,128,1,1536]{4,1,3,0,2:T(2,128)(2,1)} %copy.72), calls=%async_computation.2 | async-start | bytes 1572864 | tf_op jit(solution)/shard_map/all_to_all | solution.py:54
  99.5 90.5 %reduce-scatter.2.cloned.1.call-start = ((), (), s32[]{:S(2)}) async-start(), calls=%async_computation.6 | async-start | bytes 4718592 | tf_op jit(solution)/shard_map/reduce_scatter | solution.py:89
  122.8 1.4 copy-start
Sparse Core Ops, SparseCore 0:
  11.0 154.2 all-gather.1
  173.5 16.4 reduce-scatter.1
where the time goes:
time: 200 us; the launch traced here: 199 us
  waiting for transfers between devices  91.4 us (46%)
  blocking collectives  35.6 us (18%)
  starting transfers between devices  29.5 us (15%)
  local copies, waits for them, and re-layouts  14.2 us (7%)
  between operations  13.6 us (7%)
  matrix products  10.2 us (5%)
  other arithmetic  4.75 us (2%)
    all_to_all x1, blocking collectives, per_device(): lax.all_to_all(temporal.reshape(groups, frames_dev, 1, patch_dev, feats),...  35.6 us
    all_to_all x1, waiting for transfers between devices, per_device(): lax.all_to_all(q_frames.reshape(wide), ('grp', 'sp'), split_axis=2, conca...  26.1 us
    all_to_all x1, waiting for transfers between devices, per_device(): lax.all_to_all(spatial.reshape(wide), ('grp', 'sp'), split_axis=2, concat...  24.6 us
    all_to_all x1, waiting for transfers between devices, per_device(): lax.all_to_all(k_frames.reshape(wide), ('grp', 'sp'), split_axis=2, conca...  19.8 us
    reduce_scatter x1, waiting for transfers between devices, per_device(): lax.psum_scatter(partial_rows, 'tp', scatter_dimension=1, tiled=True)  16.7 us
    all_to_all x1, starting transfers between devices, per_device(): lax.all_to_all(spatial.reshape(wide), ('grp', 'sp'), split_axis=2, concat...  16.3 us
    dot_general x1, matrix products, per_device(): jnp.dot(tmix, lax.all_gather(out_weight, ('grp', 'sp'), axis=1, tiled=Tru...  7.99 us
    all_to_all x1, starting transfers between devices, per_device(): lax.all_to_all(k_frames.reshape(wide), ('grp', 'sp'), split_axis=2, conca...  6.77 us
  transfers between devices with their start and end apart: 5, of which 5 were waited for; matrix products, arithmetic and copies ran while one was open for 9% of the time, Pallas kernels for 0%

commit v1 on v0

v1 whole, which is shorter than its diff:
```python
import functools

import jax
import jax.numpy as jnp
from jax import lax
from jax.experimental import pallas as pl
from jax.experimental.pallas import tpu as pltpu
from jax.sharding import PartitionSpec as P

MESH = pl.DeviceIdType.MESH
HD = 128
PMAX = 128
NY, NX, NZ = 4, 4, 8
GROUPS = NY * NX * NZ
F32 = jnp.float32
BF16 = jnp.bfloat16
NT = (((1,), (1,)), ((), ()))
NN = (((1,), (0,)), ((), ()))


def softmax_rows(scores, mask):
    masked = jnp.where(mask, scores, F32(-1e30))
    top = jnp.max(masked, axis=-1, keepdims=True)
    expo = jnp.exp(masked - top)
    return (expo / jnp.sum(expo, axis=-1, keepdims=True)).astype(BF16)


def kernel(
    heads,
    qs, ks, vs, qt, kt, w, fv_col, fv_row, patches,
    out,
    stage, qk_send, qk_recv, v_send, v_recv, o_send, o_recv, weights, mixed_in, wa, wb, wfull, part, part_recv, own,
    sem_qk, sem_v, sem_o, sem_part_s, sem_part_r, sem_wz_s, sem_wz_r, sem_w1_s, sem_w1_r, sem_w2_s, sem_w2_r,
):
    grp = lax.axis_index("grp")
    z = lax.axis_index("sp")
    core = lax.axis_index("tp")
    y, x = grp // NX, grp % NX
    me = grp * NZ + z
    rows = 2 * heads
    cols = w.shape[1]
    half = heads * HD // 2

    def peer(i):
        dy, dx, dz = i // (NX * NZ), (i // NZ) % NX, i % NZ
        g2 = ((y + dy) % NY) * NX + (x + dx) % NX
        return g2, (z + dz) % NZ

    def at_x(d):
        return {"grp": y * NX + (x + d + NX) % NX}

    def at_y(d):
        return {"grp": ((y + d + NY) % NY) * NX + x}

    def at_z(d):
        return {"sp": (z + d + NZ) % NZ}

    barrier = pltpu.get_barrier_semaphore()

    def greet(i, carry):
        g2, s2 = peer(i)
        pl.semaphore_signal(barrier, inc=1, device_id={"grp": g2, "sp": s2}, device_id_type=MESH)
        return carry

    lax.fori_loop(1, GROUPS, greet, 0)
    pl.semaphore_signal(barrier, inc=1, device_id={"tp": 1 - core}, device_id_type=MESH)

    eye = (
        lax.broadcasted_iota(jnp.int32, (cols, cols), 0) == lax.broadcasted_iota(jnp.int32, (cols, cols), 1)
    ).astype(BF16)
    turned = lax.dot_general(eye, w[...], NT, preferred_element_type=F32).astype(BF16)
    wa[x, y, z] = turned[:, :half]
    wb[y, x, z] = turned[:, half:]

    def to_stage(value, frame, head, base, height):
        stage[pl.ds(base + frame * heads + head, PMAX, stride=height), :] = value.astype(F32)

    def to_chunks(dst, height):
        def body(i, carry):
            block = stage[pl.ds(pl.multiple_of(i * 16 * height, 16), 16 * height), :]
            dst[pl.ds(i * 16, 16)] = block.reshape(16, height, HD).astype(BF16)
            return carry

        lax.fori_loop(0, GROUPS // 16, body, 0)

    def from_chunks(src, height):
        def body(i, carry):
            block = src[pl.ds(i * 16, 16)].astype(F32)
            stage[pl.ds(pl.multiple_of(i * 16 * height, 16), 16 * height), :] = block.reshape(16 * height, HD)
            return carry

        lax.fori_loop(0, GROUPS // 16, body, 0)

    def head_rows(frame, head, base, height):
        return stage[pl.ds(base + frame * heads + head, PMAX, stride=height), :]

    for n, src in enumerate((qt, kt)):
        for f in range(2):
            for h in range(heads):
                to_stage(src[f * PMAX : (f + 1) * PMAX, h * HD : (h + 1) * HD], f, h, n * rows, 2 * rows)
    to_chunks(qk_send, 2 * rows)

    pl.semaphore_wait(barrier, GROUPS)

    def w_copy(src, dst, send, recv, where):
        return pltpu.make_async_remote_copy(
            src_ref=src, dst_ref=dst, send_sem=send, recv_sem=recv, device_id=where, device_id_type=MESH
        )

    def z_copies(step, sign):
        zz = (z - sign * step + NZ) % NZ
        lane = 0 if sign > 0 else 1
        spot = [lane, step]
        return [
            w_copy(wa.at[x, y, zz], wa.at[x, y, zz], sem_wz_s.at[0, lane, step], sem_wz_r.at[0, lane, step], at_z(sign)),
            w_copy(wb.at[y, x, zz], wb.at[y, x, zz], sem_wz_s.at[1, lane, step], sem_wz_r.at[1, lane, step], at_z(sign)),
        ]

    z_plan = [(0, 1), (0, -1), (1, 1), (1, -1), (2, 1), (2, -1), (3, 1)]
    for step, sign in z_plan[:2]:
        for c in z_copies(step, sign):
            c.start()

    def exchange(send_buf, recv_buf, sems):
        def copy(i):
            g2, s2 = peer(i)
            return pltpu.make_async_remote_copy(
                src_ref=send_buf.at[g2 * NZ + s2], dst_ref=recv_buf.at[me], send_sem=sems.at[0], recv_sem=sems.at[1],
                device_id={"grp": g2, "sp": s2}, device_id_type=MESH,
            )

        def body(i, carry):
            copy(i).start()
            return carry

        lax.fori_loop(1, GROUPS, body, 0)
        recv_buf[me] = send_buf[me]

        return pltpu.make_async_remote_copy(
            src_ref=send_buf.at[pl.ds(0, GROUPS - 1)], dst_ref=recv_buf.at[pl.ds(0, GROUPS - 1)],
            send_sem=sems.at[0], recv_sem=sems.at[1], device_id={"tp": core}, device_id_type=MESH,
        )

    sent_qk = exchange(qk_send, qk_recv, sem_qk)

    scale = F32(HD**-0.5)
    key_at = lax.broadcasted_iota(jnp.int32, (PMAX, PMAX), 1)

    for f in range(2):
        for h in range(heads):
            at = (slice(f * PMAX, (f + 1) * PMAX), slice(h * HD, (h + 1) * HD))
            scores = lax.dot_general(qs[at], ks[at], NT, preferred_element_type=F32) * scale
            probs = softmax_rows(scores, key_at < patches[f])
            value = lax.dot_general(probs, vs[at], NN, preferred_element_type=F32)
            to_stage(value.astype(BF16), f, h, 0, rows)
    to_chunks(v_send, rows)
    sent_v = exchange(v_send, v_recv, sem_v)

    for n, (step, sign) in enumerate(z_plan):
        for c in z_copies(step, sign):
            c.wait_recv()
        if n + 2 < len(z_plan):
            for c in z_copies(*z_plan[n + 2]):
                c.start()

    def first_copies(sign):
        lane = 0 if sign > 0 else 1
        return [
            w_copy(wa.at[x, y], wa.at[x, y], sem_w1_s.at[0, lane], sem_w1_r.at[0, lane], at_y(sign)),
            w_copy(wb.at[y, x], wb.at[y, x], sem_w1_s.at[1, lane], sem_w1_r.at[1, lane], at_x(sign)),
        ]

    def first_forward(sign):
        lane = 2 if sign > 0 else 3
        part_z = pl.ds(0, NZ // 2) if sign > 0 else pl.ds(NZ // 2, NZ // 2)
        yy, xx = (y - sign + NY) % NY, (x - sign + NX) % NX
        return [
            w_copy(wa.at[x, yy, part_z], wa.at[x, yy, part_z], sem_w1_s.at[0, lane], sem_w1_r.at[0, lane], at_y(sign)),
            w_copy(wb.at[y, xx, part_z], wb.at[y, xx, part_z], sem_w1_s.at[1, lane], sem_w1_r.at[1, lane], at_x(sign)),
        ]

    for sign in (1, -1):
        for c in first_copies(sign):
            c.start()
    for sign in (1, -1):
        for c in first_copies(sign):
            c.wait_recv()
        for c in first_forward(sign):
            c.start()

    def second_copies(sign, j):
        lane = 0 if sign > 0 else 1
        return [
            w_copy(wa.at[x, j], wa.at[x, j], sem_w2_s.at[0, lane, j], sem_w2_r.at[0, lane, j], at_x(sign)),
            w_copy(wb.at[y, j], wb.at[y, j], sem_w2_s.at[1, lane, j], sem_w2_r.at[1, lane, j], at_y(sign)),
        ]

    def second_forward(sign, j):
        lane = 2 if sign > 0 else 3
        yy, xx = (y - sign + NY) % NY, (x - sign + NX) % NX
        return [
            w_copy(wa.at[xx, j], wa.at[xx, j], sem_w2_s.at[0, lane, j], sem_w2_r.at[0, lane, j], at_x(sign)),
            w_copy(wb.at[yy, j], wb.at[yy, j], sem_w2_s.at[1, lane, j], sem_w2_r.at[1, lane, j], at_y(sign)),
        ]

    for sign in (1, -1):
        for c in first_forward(sign):
            c.wait_recv()
    for j in range(4):
        for sign in (1, -1):
            for c in second_copies(sign, j):
                c.start()

    sent_qk.wait_recv()
    from_chunks(qk_recv, 2 * rows)
    same = fv_col[...] == fv_row[...]
    for h in range(heads):
        q = jnp.concatenate([head_rows(f, h, 0, 2 * rows) for f in range(2)], axis=0).astype(BF16)
        k = jnp.concatenate([head_rows(f, h, rows, 2 * rows) for f in range(2)], axis=0).astype(BF16)
        scores = lax.dot_general(q, k, NT, preferred_element_type=F32) * scale
        weights[h] = softmax_rows(scores, same)

    for j in range(4):
        for sign in (1, -1):
            for c in second_copies(sign, j):
                c.wait_recv()
            if (j < 2) == (sign > 0):
                for c in second_forward(sign, j):
                    c.start()

    sent_v.wait_recv()
    from_chunks(v_recv, rows)
    for h in range(heads):
        v = jnp.concatenate([head_rows(f, h, 0, rows) for f in range(2)], axis=0).astype(BF16)
        value = lax.dot_general(weights[h], v, NN, preferred_element_type=F32)
        mixed_in[:, h * HD : (h + 1) * HD] = value.astype(BF16)

    for sign in (1, -1):
        for j in range(4):
            if (j < 2) == (sign > 0):
                for c in second_forward(sign, j):
                    c.wait_recv()

    def repack(i, carry):
        yy, xx = i // NX, i % NX
        at = pl.ds(pl.multiple_of(i * NZ * cols, 16), NZ * cols)
        wfull[at, :half] = wa[xx, yy].astype(F32).reshape(NZ * cols, half).astype(BF16)
        wfull[at, half:] = wb[yy, xx].astype(F32).reshape(NZ * cols, half).astype(BF16)
        return carry

    lax.fori_loop(0, NY * NX, repack, 0)

    blocks, _, width = part.shape
    mine = blocks * width

    def product(first, i):
        at = pl.ds(pl.multiple_of(first * mine + i * width, 16), width)
        return lax.dot_general(mixed_in[...], wfull[at, :], NT, preferred_element_type=F32)

    def part_copy(i):
        return pltpu.make_async_remote_copy(
            src_ref=part.at[i], dst_ref=part_recv.at[i], send_sem=sem_part_s.at[i], recv_sem=sem_part_r.at[i],
            device_id={"tp": 1 - core}, device_id_type=MESH,
        )

    def give(i, carry):
        part[i] = product(1 - core, i)
        part_copy(i).start()
        return carry

    lax.fori_loop(0, blocks, give, 0)

    def keep(i, carry):
        own[i] = product(core, i)
        return carry

    lax.fori_loop(0, blocks, keep, 0)
    for i in range(blocks):
        part_copy(i).wait_recv()
        total = own[i] + part_recv[i]
        for f in range(2):
            for j in range(width // HD):
                to_stage(total[f * PMAX : (f + 1) * PMAX, j * HD : (j + 1) * HD], f, i * (width // HD) + j, 0, rows)
    to_chunks(o_send, rows)
    sent_o = exchange(o_send, o_recv, sem_o)

    sent_qk.wait_send()
    sent_v.wait_send()
    for i in range(blocks):
        part_copy(i).wait_send()
    for step, sign in z_plan:
        for c in z_copies(step, sign):
            c.wait_send()
    for sign in (1, -1):
        for c in first_copies(sign) + first_forward(sign):
            c.wait_send()
        for j in range(4):
            for c in second_copies(sign, j):
                c.wait_send()
            if (j < 2) == (sign > 0):
                for c in second_forward(sign, j):
                    c.wait_send()

    sent_o.wait_recv()
    from_chunks(o_recv, rows)
    row_at = lax.broadcasted_iota(jnp.int32, (PMAX, HD), 0)
    for f in range(2):
        alive = row_at < patches[f]
        for h in range(heads):
            value = jnp.where(alive, head_rows(f, h, 0, rows), F32(0.0))
            out[f * PMAX : (f + 1) * PMAX, h * HD : (h + 1) * HD] = value.astype(BF16)
    sent_o.wait_send()


def per_device(q_spatial, k_spatial, v_spatial, q_temporal, k_temporal, out_weight, frame_video, video_patches):
    rows, feats = q_spatial.shape
    heads = feats // HD
    cols = out_weight.shape[1]
    frames = rows // PMAX
    first = lax.axis_index(("grp", "sp")) * frames
    my_video = lax.dynamic_slice_in_dim(frame_video, first, frames)
    match = my_video[:, None] == jnp.arange(video_patches.shape[0], dtype=jnp.int32)[None, :]
    patches = jnp.sum(jnp.where(match, video_patches[None, :], 0), axis=1).astype(jnp.int32)
    by_slot = frame_video.reshape(GROUPS, frames).T.reshape(-1)
    vmem = pl.BlockSpec(memory_space=pltpu.VMEM)
    chunk = frames * heads
    blocks = 4
    width = feats // blocks
    all_frames = frame_video.shape[0]
    dma = pltpu.SemaphoreType.DMA
    return pl.pallas_call(
        functools.partial(kernel, heads),
        out_shape=jax.ShapeDtypeStruct((rows, feats), BF16),
        in_specs=[vmem] * 8 + [pl.BlockSpec(memory_space=pltpu.SMEM)],
        out_specs=vmem,
        scratch_shapes=[
            pltpu.VMEM((GROUPS * 2 * chunk, HD), F32),
            pltpu.VMEM((GROUPS, 2 * chunk, HD), BF16),
            pltpu.VMEM((GROUPS, 2 * chunk, HD), BF16),
            pltpu.VMEM((GROUPS, chunk, HD), BF16),
            pltpu.VMEM((GROUPS, chunk, HD), BF16),
            pltpu.VMEM((GROUPS, chunk, HD), BF16),
            pltpu.VMEM((GROUPS, chunk, HD), BF16),
            pltpu.VMEM((heads, all_frames, all_frames), BF16),
            pltpu.VMEM((all_frames, feats), BF16),
            pltpu.VMEM((NX, NY, NZ, cols, feats // 2), BF16),
            pltpu.VMEM((NY, NX, NZ, cols, feats // 2), BF16),
            pltpu.VMEM((GROUPS * cols, feats), BF16),
            pltpu.VMEM((blocks, all_frames, width), F32),
            pltpu.VMEM((blocks, all_frames, width), F32),
            pltpu.VMEM((blocks, all_frames, width), F32),
            dma((2,)),
            dma((2,)),
            dma((2,)),
            dma((blocks,)),
            dma((blocks,)),
            dma((2, 2, 4)),
            dma((2, 2, 4)),
            dma((2, 4)),
            dma((2, 4)),
            dma((2, 4, 4)),
            dma((2, 4, 4)),
        ],
        compiler_params=pltpu.CompilerParams(
            collective_id=0, has_side_effects=True, vmem_limit_bytes=58 * 2**20
        ),
    )(
        q_spatial, k_spatial, v_spatial, q_temporal, k_temporal, out_weight,
        by_slot[:, None], by_slot[None, :], patches,
    )


def solution(mesh):
    return jax.shard_map(
        per_device,
        mesh=mesh,
        in_specs=(
            P(("grp", "sp"), "tp"),
            P(("grp", "sp"), "tp"),
            P(("grp", "sp"), "tp"),
            P(("grp", "sp"), "tp"),
            P(("grp", "sp"), "tp"),
            P("tp", ("grp", "sp")),
            P(),
            P(),
        ),
        out_specs=P(("grp", "sp"), "tp"),
        check_vma=False,
    )
```

time: 200 us -> 164 us (0.82)
  Pallas kernels: 0 us -> 157 us
  waiting for transfers between devices: 91.4 us -> 0 us
  blocking collectives: 35.6 us -> 0 us
  starting transfers between devices: 29.5 us -> 0 us
  between operations: 13.6 us -> 0.02 us
  matrix products: 10.2 us -> 0 us
  local copies, waits for them, and re-layouts: 14.2 us -> 5.9 us
  other arithmetic: 4.75 us -> 0.72 us
    pallas_call x0 -> x1, Pallas kernels: none -> 157 us  [per_device(): pl.pallas_call(functools.partial(kernel, heads), out_shape=jax.ShapeDtype...]
    all_to_all x3 -> x0, waiting for transfers between devices: 70.4 us -> none  [the longest x1 26.1 us: per_device(): lax.all_to_all(q_frames.reshape(wide), ('grp', 'sp'), split_axis=2, conca...]
    all_to_all x1 -> x0, blocking collectives: 35.6 us -> none  [per_device(): lax.all_to_all(temporal.reshape(groups, frames_dev, 1, patch_dev, feats),...]
    all_to_all x3 -> x0, starting transfers between devices: 29.3 us -> none  [the longest x1 16.3 us: per_device(): lax.all_to_all(spatial.reshape(wide), ('grp', 'sp'), split_axis=2, concat...]
    reduce_scatter x1 -> x0, waiting for transfers between devices: 16.7 us -> none  [per_device(): lax.psum_scatter(partial_rows, 'tp', scatter_dimension=1, tiled=True)]
    dot_general x5 -> x0, matrix products: 10.2 us -> none  [the longest x1 7.99 us: per_device(): jnp.dot(tmix, lax.all_gather(out_weight, ('grp', 'sp'), axis=1, tiled=Tru...]
    another operation x6 -> x1, local copies, waits for them, and re-layouts: 7.72 us -> 0.79 us  [per_device(): by_slot[:, None]]
    reshape x4 -> x1, local copies, waits for them, and re-layouts: 5.28 us -> 0.13 us  [per_device(): by_slot = frame_video.reshape(GROUPS, frames).T.reshape(-1)]
  transfers between devices with their start and end apart: 5 -> 0, of which waited for: 5 -> 0; matrix products, arithmetic and copies ran while one was open for 9% -> 0% of each run, Pallas kernels for 0% -> 0%
where the time goes in v1:
time: 164 us
  Pallas kernels  157 us (96%)
  local copies, waits for them, and re-layouts  5.9 us (4%)
    pallas_call x1, Pallas kernels, per_device(): pl.pallas_call(functools.partial(kernel, heads), out_shape=jax.ShapeDtype...  157 us
    unnamed x10, local copies, waits for them, and re-layouts  4.84 us

profile of v1, /device:TPU:1, one launch (start us, length us, event | category | flops | bytes accessed | tf_op | source)
XLA Modules:
  0.0 163.7 jit_solution(16084742855860061049)
XLA Ops:
  0.0 0.0 copy-start.2
  0.0 0.7 copy-done.2
  0.7 0.0 copy-start.3
  0.7 0.1 dynamic_slice.3
  0.8 0.6 copy-done.3
  1.3 0.7 fusion.patches
  2.1 0.1 reshape.5
  2.2 0.1 copy.14
  2.3 0.0 copy-start.1
  2.3 0.0 copy-start
  2.3 0.6 copy-done.1
  2.9 0.8 copy.17.fv_col
  3.6 0.0 copy-done
  3.7 0.9 copy.16.w
  4.6 157.1 %shard_map.82 = bf16[256,1536]{1,0:T(8,128)(2,1)} custom-call(bf16[256,1536]{1,0:T(8,128)(2,1)} %qs.1, bf16[256,1536]{1,0:T(8,128)(2,1)} %ks.1, bf16[256,1536]{1,0:T(8,128)(2,1)} %vs.1, bf16[256,1536]{1,0:T(8,128)(2,1)} %qt.1, bf16[256,1536]{1,0:T(8,128)(2,1)} %kt.1, bf16[1536,24]{1,0:T(8,128)(2,1)} %copy.16.w, s32[256,1]{1,0:T(8,128)} %copy.17.fv_col, ...), custom_call_target="tpu_custom_call" | custom-call | tf_op jit(solution)/shard_map/pallas_call | solution.py:331
  161.7 2.1 %copy.19 = bf16[256,1536]{1,0:T(8,128)(2,1)} copy(bf16[256,1536]{1,0:T(8,128)(2,1)} %shard_map.82) | data formatting | bytes 1572864
Async XLA Ops:
  0.0 0.7 copy-start.2
  0.7 0.7 copy-start.3
  2.3 0.6 copy-start.1
  2.3 1.4 copy-start

commit v2 on v0

v2 whole, which is shorter than its diff:
```python
import functools

import jax
import jax.numpy as jnp
from jax import lax
from jax.experimental import pallas as pl
from jax.experimental.pallas import tpu as pltpu
from jax.sharding import PartitionSpec as P

MESH = pl.DeviceIdType.MESH
HD = 128
PMAX = 128
NY, NX, NZ = 4, 4, 8
GROUPS = NY * NX * NZ
PARTS = 3
F32 = jnp.float32
BF16 = jnp.bfloat16
NT = (((1,), (1,)), ((), ()))
NN = (((1,), (0,)), ((), ()))


def softmax_rows(scores, mask):
    masked = jnp.where(mask, scores, F32(-1e30))
    top = jnp.max(masked, axis=-1, keepdims=True)
    expo = jnp.exp(masked - top)
    return (expo / jnp.sum(expo, axis=-1, keepdims=True)).astype(BF16)


def kernel(
    heads, parts,
    qs, ks, vs, qt, kt, w, fv_col, fv_row, patches,
    out,
    stage, f_send, f_recv, o_send, o_recv, tall, wy, wfull, part, part_recv, own,
    sem_f, sem_o, sem_t_s, sem_t_r, sem_part_s, sem_part_r, sem_wz_s, sem_wz_r, sem_wy_s, sem_wy_r,
):
    grp = lax.axis_index("grp")
    z = lax.axis_index("sp")
    core = lax.axis_index("tp")
    y, x = grp // NX, grp % NX
    me = grp * NZ + z
    cols = w.shape[1]
    per = heads // parts
    height = f_send.shape[2]

    def peer(i):
        dy, dx, dz = i // (NX * NZ), (i // NZ) % NX, i % NZ
        g2 = ((y + dy) % NY) * NX + (x + dx) % NX
        return g2, (z + dz) % NZ

    barrier = pltpu.get_barrier_semaphore()

    def greet(i, carry):
        g2, s2 = peer(i)
        pl.semaphore_signal(barrier, inc=1, device_id={"grp": g2, "sp": s2}, device_id_type=MESH)
        return carry

    lax.fori_loop(1, GROUPS, greet, 0)
    pl.semaphore_signal(barrier, inc=1, device_id={"tp": 1 - core}, device_id_type=MESH)

    def remote(src, dst, send, recv, where):
        return pltpu.make_async_remote_copy(
            src_ref=src, dst_ref=dst, send_sem=send, recv_sem=recv, device_id=where, device_id_type=MESH
        )

    eye = (
        lax.broadcasted_iota(jnp.int32, (cols, cols), 0) == lax.broadcasted_iota(jnp.int32, (cols, cols), 1)
    ).astype(BF16)
    wy[y, z] = lax.dot_general(eye, w[...], NT, preferred_element_type=F32).astype(BF16)

    scale = F32(HD**-0.5)
    key_at = lax.broadcasted_iota(jnp.int32, (PMAX, PMAX), 1)

    def build(n):
        for f in range(2):
            rows = slice(f * PMAX, (f + 1) * PMAX)
            for j in range(per):
                at = (rows, slice((n * per + j) * HD, (n * per + j + 1) * HD))
                scores = lax.dot_general(qs[at], ks[at], NT, preferred_element_type=F32) * scale
                probs = softmax_rows(scores, key_at < patches[f])
                value = lax.dot_general(probs, vs[at], NN, preferred_element_type=F32)
                spot = f * per + j
                stage[pl.ds(spot, PMAX, stride=height), :] = qt[at].astype(F32)
                stage[pl.ds(2 * per + spot, PMAX, stride=height), :] = kt[at].astype(F32)
                stage[pl.ds(4 * per + spot, PMAX, stride=height), :] = value

        def pack(i, carry):
            block = stage[pl.ds(pl.multiple_of(i * 16 * height, 16), 16 * height), :]
            f_send[n, pl.ds(i * 16, 16)] = block.reshape(16, height, HD).astype(BF16)
            return carry

        lax.fori_loop(0, GROUPS // 16, pack, 0)

    def unpack(src):
        def body(i, carry):
            block = src[pl.ds(i * 16, 16)].astype(F32)
            stage[pl.ds(pl.multiple_of(i * 16 * height, 16), 16 * height), :] = block.reshape(16 * height, HD)
            return carry

        lax.fori_loop(0, GROUPS // 16, body, 0)

    def exchange(send_buf, recv_buf, sems, first, last):
        def body(i, carry):
            g2, s2 = peer(i)
            remote(send_buf.at[g2 * NZ + s2], recv_buf.at[me], sems.at[0], sems.at[1], {"grp": g2, "sp": s2}).start()
            return carry

        lax.fori_loop(first, last, body, 0)

    def exchanged(send_buf, recv_buf, sems):
        rest = pl.ds(0, GROUPS - 1)
        return remote(send_buf.at[rest], recv_buf.at[rest], sems.at[0], sems.at[1], {"tp": core})

    def z_copy(d):
        return remote(wy.at[y, z], wy.at[y, z], sem_wz_s.at[d], sem_wz_r.at[d], {"sp": (z + d) % NZ})

    def y_copy(e, d):
        zz = (z - e + NZ) % NZ
        return remote(
            wy.at[y, zz], wy.at[y, zz], sem_wy_s.at[e, d - 1], sem_wy_r.at[e, d - 1],
            {"grp": ((y + d) % NY) * NX + x},
        )

    def t_copy(n, k, d):
        at = (y + k) % NY
        return remote(
            tall.at[n, x, at], tall.at[n, x, at], sem_t_s.at[n, k, d - 1], sem_t_r.at[n, k, d - 1],
            {"grp": y * NX + (x + d) % NX},
        )

    z_order = (0, 1, 7, 2, 6, 3, 5, 4)
    around = (1, 3, 2)
    plane = NX * NZ

    build(0)
    pl.semaphore_wait(barrier, GROUPS)
    for e in (4, 3, 5, 2, 6, 1, 7):
        z_copy(e).start()
    exchange(f_send.at[0], f_recv.at[0], sem_f.at[0], 1, GROUPS)
    build(1)
    for n, e in enumerate(z_order):
        if e > 0:
            z_copy(e).wait_recv()
        for d in around:
            y_copy(e, d).start()
        first = n * (GROUPS // NZ)
        exchange(f_send.at[1], f_recv.at[1], sem_f.at[1], max(first, 1), first + GROUPS // NZ)
    build(2)
    exchange(f_send.at[2], f_recv.at[2], sem_f.at[2], 1, GROUPS)
    for n in range(parts):
        f_recv[n, me] = f_send[n, me]

    odd = x % 2
    third = NZ * cols
    small = third // 3

    def order_weights():
        for e in z_order:
            for d in around:
                y_copy(e, d).wait_recv()
        for yy in range(NY):
            block = wy[yy].astype(F32).reshape(third, heads * HD)
            base = (yy // 2) * 2 * third
            big = jnp.where(odd == 0, block[: 2 * small], block[small:]).astype(BF16)
            wfull[base + (yy % 2) * 2 * small : base + (yy % 2 + 1) * 2 * small, :] = big
            rest = jnp.where(odd == 0, block[2 * small :], block[:small]).astype(BF16)
            spot = odd + (yy % 2) - 2 * odd * (yy % 2)
            wfull[pl.ds(pl.multiple_of(base + 4 * small + spot * small, 16), small), :] = rest

    same = fv_col[...] == fv_row[...]
    for n in range(parts):
        if n == parts - 1:
            order_weights()
        exchanged(f_send.at[n], f_recv.at[n], sem_f.at[n]).wait_recv()
        unpack(f_recv.at[n])
        for j in range(per):
            q, k, v = (
                jnp.concatenate(
                    [stage[pl.ds(t * 2 * per + f * per + j, GROUPS, stride=height), :] for f in range(2)], axis=0
                ).astype(BF16)
                for t in range(3)
            )
            scores = lax.dot_general(q, k, NT, preferred_element_type=F32) * scale
            probs = softmax_rows(scores, same)
            value = lax.dot_general(probs, v, NN, preferred_element_type=F32)
            for k in range(NY):
                for f in range(2):
                    rows = value[f * GROUPS + k * plane : f * GROUPS + (k + 1) * plane]
                    tall[n, x, k, f * plane : (f + 1) * plane, j * HD : (j + 1) * HD] = rows.astype(BF16)
        for k in range(NY):
            for d in around:
                t_copy(n, k, d).start()

    width = 2 * third
    feats = per * HD

    def product(k, c):
        total = None
        for n in range(parts):
            left = jnp.concatenate([tall[n, s, (y + k) % NY] for s in range(NX)], axis=0)
            right = wfull[pl.ds(pl.multiple_of(c * width, 16), width), n * feats : (n + 1) * feats]
            term = lax.dot_general(left, right, NT, preferred_element_type=F32)
            total = term if total is None else total + term
        return total

    def part_copy(k):
        return remote(part.at[k], part_recv.at[k], sem_part_s.at[k], sem_part_r.at[k], {"tp": 1 - core})

    for k in range(NY):
        for n in range(parts):
            for d in around:
                t_copy(n, k, d).wait_recv()
        part[k] = product(k, 1 - core)
        part_copy(k).start()
        own[k] = product(k, core)
        part_copy(k).wait_recv()
        total = own[k] + part_recv[k]
        for s in range(NX):
            for f in range(2):
                for j in range(width // HD):
                    stage[pl.ds((s * 2 + f) * (width // HD) + j, plane, stride=height), :] = total[
                        (s * 2 + f) * plane : (s * 2 + f + 1) * plane, j * HD : (j + 1) * HD
                    ]
        for i in range(plane // 16):
            block = stage[i * 16 * height : (i + 1) * 16 * height, :]
            o_send[pl.ds(((y + k) % NY) * plane + i * 16, 16)] = block.reshape(16, height, HD).astype(BF16)
        exchange(o_send, o_recv, sem_o, max(k * plane, 1), (k + 1) * plane)
        if k == 0:
            o_recv[me] = o_send[me]

    for n in range(parts):
        exchanged(f_send.at[n], f_recv.at[n], sem_f.at[n]).wait_send()
        for k in range(NY):
            for d in around:
                t_copy(n, k, d).wait_send()
    for k in range(NY):
        part_copy(k).wait_send()
    for e in z_order:
        if e > 0:
            z_copy(e).wait_send()
        for d in around:
            y_copy(e, d).wait_send()

    done = exchanged(o_send, o_recv, sem_o)
    done.wait_recv()
    unpack(o_recv)
    row_at = lax.broadcasted_iota(jnp.int32, (plane, HD), 0)
    low = lax.broadcasted_iota(jnp.int32, (plane, HD), 1) < HD // 2

    def finish(yy, carry):
        for f in range(2):
            alive = row_at + yy * plane < patches[f]

            def piece(xx, j):
                return jnp.concatenate(
                    [stage[pl.ds(((yy * NX + xx) * NZ) * height + (s * 2 + f) * (width // HD) + j, NZ, stride=height), :]
                     for s in range(NX)], axis=0)

            def put(at, value):
                rows = pl.ds(pl.multiple_of(f * PMAX + yy * plane, plane), plane)
                out[rows, at * HD : (at + 1) * HD] = jnp.where(alive, value, F32(0.0)).astype(BF16)

            for m in range(NX // 2):
                left, right = piece(2 * m, 2), piece(2 * m + 1, 2)
                middle = (
                    jnp.where(low, left, right),
                    pltpu.roll(jnp.where(low, right, left), HD // 2, 1),
                )
                for half in range(2):
                    at = half * (NX * third // HD) + m * (2 * third // HD)
                    put(at, piece(2 * m, half))
                    put(at + 1, middle[half])
                    put(at + 2, piece(2 * m + 1, half))
        return carry

    lax.fori_loop(0, NY, finish, 0)
    done.wait_send()


def per_device(q_spatial, k_spatial, v_spatial, q_temporal, k_temporal, out_weight, frame_video, video_patches):
    rows, feats = q_spatial.shape
    heads = feats // HD
    cols = out_weight.shape[1]
    frames = rows // PMAX
    first = lax.axis_index(("grp", "sp")) * frames
    my_video = lax.dynamic_slice_in_dim(frame_video, first, frames)
    match = my_video[:, None] == jnp.arange(video_patches.shape[0], dtype=jnp.int32)[None, :]
    patches = jnp.sum(jnp.where(match, video_patches[None, :], 0), axis=1).astype(jnp.int32)
    by_slot = frame_video.reshape(GROUPS, frames).T.reshape(-1)
    vmem = pl.BlockSpec(memory_space=pltpu.VMEM)
    parts = PARTS
    height = 3 * frames * heads // parts
    all_frames = frame_video.shape[0]
    width = 2 * NZ * cols
    dma = pltpu.SemaphoreType.DMA
    return pl.pallas_call(
        functools.partial(kernel, heads, parts),
        out_shape=jax.ShapeDtypeStruct((rows, feats), BF16),
        in_specs=[vmem] * 8 + [pl.BlockSpec(memory_space=pltpu.SMEM)],
        out_specs=vmem,
        scratch_shapes=[
            pltpu.VMEM((GROUPS * height, HD), F32),
            pltpu.VMEM((parts, GROUPS, height, HD), BF16),
            pltpu.VMEM((parts, GROUPS, height, HD), BF16),
            pltpu.VMEM((GROUPS, height, HD), BF16),
            pltpu.VMEM((GROUPS, height, HD), BF16),
            pltpu.VMEM((parts, NX, NY, all_frames // NY, feats // parts), BF16),
            pltpu.VMEM((NY, NZ, cols, feats), BF16),
            pltpu.VMEM((2 * width, feats), BF16),
            pltpu.VMEM((NY, all_frames, width), F32),
            pltpu.VMEM((NY, all_frames, width), F32),
            pltpu.VMEM((NY, all_frames, width), F32),
            dma((parts, 2)),
            dma((2,)),
            dma((parts, NY, 3)),
            dma((parts, NY, 3)),
            dma((NY,)),
            dma((NY,)),
            dma((NZ,)),
            dma((NZ,)),
            dma((NZ, 3)),
            dma((NZ, 3)),
        ],
        compiler_params=pltpu.CompilerParams(
            collective_id=0, has_side_effects=True, vmem_limit_bytes=58 * 2**20
        ),
    )(
        q_spatial, k_spatial, v_spatial, q_temporal, k_temporal, out_weight,
        by_slot[:, None], by_slot[None, :], patches,
    )


def solution(mesh):
    return jax.shard_map(
        per_device,
        mesh=mesh,
        in_specs=(
            P(("grp", "sp"), "tp"),
            P(("grp", "sp"), "tp"),
            P(("grp", "sp"), "tp"),
            P(("grp", "sp"), "tp"),
            P(("grp", "sp"), "tp"),
            P("tp", ("grp", "sp")),
            P(),
            P(),
        ),
        out_specs=P(("grp", "sp"), "tp"),
        check_vma=False,
    )
```

time: 200 us -> 127 us (0.64)
  Pallas kernels: 0 us -> 121 us
  waiting for transfers between devices: 91.4 us -> 0 us
  blocking collectives: 35.6 us -> 0 us
  starting transfers between devices: 29.5 us -> 0 us
  between operations: 13.6 us -> 0.02 us
  matrix products: 10.2 us -> 0 us
  local copies, waits for them, and re-layouts: 14.2 us -> 5.9 us
  other arithmetic: 4.75 us -> 0.72 us
    pallas_call x0 -> x1, Pallas kernels: none -> 121 us  [per_device(): pl.pallas_call(functools.partial(kernel, heads, parts), out_shape=jax.Sha...]
    all_to_all x3 -> x0, waiting for transfers between devices: 70.4 us -> none  [the longest x1 26.1 us: per_device(): lax.all_to_all(q_frames.reshape(wide), ('grp', 'sp'), split_axis=2, conca...]
    all_to_all x1 -> x0, blocking collectives: 35.6 us -> none  [per_device(): lax.all_to_all(temporal.reshape(groups, frames_dev, 1, patch_dev, feats),...]
    all_to_all x3 -> x0, starting transfers between devices: 29.3 us -> none  [the longest x1 16.3 us: per_device(): lax.all_to_all(spatial.reshape(wide), ('grp', 'sp'), split_axis=2, concat...]
    reduce_scatter x1 -> x0, waiting for transfers between devices: 16.7 us -> none  [per_device(): lax.psum_scatter(partial_rows, 'tp', scatter_dimension=1, tiled=True)]
    dot_general x5 -> x0, matrix products: 10.2 us -> none  [the longest x1 7.99 us: per_device(): jnp.dot(tmix, lax.all_gather(out_weight, ('grp', 'sp'), axis=1, tiled=Tru...]
    another operation x6 -> x1, local copies, waits for them, and re-layouts: 7.72 us -> 0.79 us  [per_device(): by_slot[:, None]]
    reshape x4 -> x1, local copies, waits for them, and re-layouts: 5.28 us -> 0.13 us  [per_device(): by_slot = frame_video.reshape(GROUPS, frames).T.reshape(-1)]
  transfers between devices with their start and end apart: 5 -> 0, of which waited for: 5 -> 0; matrix products, arithmetic and copies ran while one was open for 9% -> 0% of each run, Pallas kernels for 0% -> 0%
where the time goes in v2:
time: 127 us
  Pallas kernels  121 us (95%)
  local copies, waits for them, and re-layouts  5.9 us (5%)
    pallas_call x1, Pallas kernels, per_device(): pl.pallas_call(functools.partial(kernel, heads, parts), out_shape=jax.Sha...  121 us
    unnamed x10, local copies, waits for them, and re-layouts  4.84 us

profile of v2, /device:TPU:1, one launch (start us, length us, event | category | flops | bytes accessed | tf_op | source)
XLA Modules:
  0.0 127.2 jit_solution(4281785302241311601)
XLA Ops:
  0.0 0.0 copy-start.2
  0.0 0.7 copy-done.2
  0.7 0.0 copy-start.3
  0.7 0.1 dynamic_slice.3
  0.8 0.6 copy-done.3
  1.3 0.7 fusion.patches
  2.1 0.1 reshape.5
  2.2 0.1 copy.14
  2.3 0.0 copy-start.1
  2.3 0.0 copy-start
  2.3 0.6 copy-done.1
  2.9 0.8 copy.17.fv_col
  3.6 0.0 copy-done
  3.7 0.9 copy.16.w
  4.6 120.5 %shard_map.82 = bf16[256,1536]{1,0:T(8,128)(2,1)} custom-call(bf16[256,1536]{1,0:T(8,128)(2,1)} %qs.1, bf16[256,1536]{1,0:T(8,128)(2,1)} %ks.1, bf16[256,1536]{1,0:T(8,128)(2,1)} %vs.1, bf16[256,1536]{1,0:T(8,128)(2,1)} %qt.1, bf16[256,1536]{1,0:T(8,128)(2,1)} %kt.1, bf16[1536,24]{1,0:T(8,128)(2,1)} %copy.16.w, s32[256,1]{1,0:T(8,128)} %copy.17.fv_col, ...), custom_call_target="tpu_custom_call" | custom-call | tf_op jit(solution)/shard_map/pallas_call | solution.py:295
  125.1 2.1 %copy.19 = bf16[256,1536]{1,0:T(8,128)(2,1)} copy(bf16[256,1536]{1,0:T(8,128)(2,1)} %shard_map.82) | data formatting | bytes 1572864
Async XLA Ops:
  0.0 0.7 copy-start.2
  0.7 0.7 copy-start.3
  2.3 0.6 copy-start.1
  2.3 1.4 %copy-start = (bf16[1536,24]{0,1:T(8,128)(2,1)S(1)}, bf16[1536,24]{0,1:T(8,128)(2,1)}, u32[]{:S(2)}) copy-start(bf16[1536,24]{0,1:T(8,128)(2,1)} %param.13) | copy-start | bytes 221188

commit v3 on v2

v3 whole, which is shorter than its diff:
```python
import functools

import jax
import jax.numpy as jnp
from jax import lax
from jax.experimental import pallas as pl
from jax.experimental.pallas import tpu as pltpu
from jax.sharding import PartitionSpec as P

MESH = pl.DeviceIdType.MESH
HD = 128
PMAX = 128
NY, NX, NZ = 4, 4, 8
GROUPS = NY * NX * NZ
PARTS = 3
LATE = 1
F32 = jnp.float32
BF16 = jnp.bfloat16
NT = (((1,), (1,)), ((), ()))
NN = (((1,), (0,)), ((), ()))


def softmax_rows(masked):
    top = jnp.max(masked, axis=-1, keepdims=True)
    expo = jnp.exp(masked - top)
    return (expo / jnp.sum(expo, axis=-1, keepdims=True)).astype(BF16)


def kernel(
    heads, parts,
    qs_hbm, ks_hbm, vs_hbm, qt_hbm, kt_hbm, w_hbm, videos, frame_video, video_patches,
    out_hbm,
    qs, ks, vs, qt, kt, out, bias, stage, f_send, f_recv, o_send, o_recv, tall, wy, wfull, part, part_recv, own,
    sem_in, sem_out, sem_f, sem_o, sem_t_s, sem_t_r, sem_part_s, sem_part_r, sem_wz_s, sem_wz_r, sem_wy_s, sem_wy_r,
):
    grp = lax.axis_index("grp")
    z = lax.axis_index("sp")
    core = lax.axis_index("tp")
    y, x = grp // NX, grp % NX
    me = grp * NZ + z
    cols = w_hbm.shape[0]
    per = heads // parts
    height = f_send.shape[2]
    plane = NX * NZ

    def load(n, j):
        src, dst = ((qs_hbm, qs), (ks_hbm, ks), (vs_hbm, vs), (qt_hbm, qt), (kt_hbm, kt))[j]
        at = pl.ds(n * per * HD, per * HD)
        return pltpu.make_async_copy(src.at[:, at], dst.at[:, at], sem_in.at[n, j])

    load_w = pltpu.make_async_copy(w_hbm, wy.at[y, z], sem_in.at[parts, 0])
    load_w.start()
    for n in range(parts):
        for j in range(5):
            load(n, j).start()

    def peer(i):
        dy, dx, dz = i // (NX * NZ), (i // NZ) % NX, i % NZ
        g2 = ((y + dy) % NY) * NX + (x + dx) % NX
        return g2, (z + dz) % NZ

    barrier = pltpu.get_barrier_semaphore()

    def greet(i, carry):
        g2, s2 = peer(i)
        pl.semaphore_signal(barrier, inc=1, device_id={"grp": g2, "sp": s2}, device_id_type=MESH)
        return carry

    lax.fori_loop(1, GROUPS, greet, 0)
    pl.semaphore_signal(barrier, inc=1, device_id={"tp": 1 - core}, device_id_type=MESH)

    def remote(src, dst, send, recv, where):
        return pltpu.make_async_remote_copy(
            src_ref=src, dst_ref=dst, send_sem=send, recv_sem=recv, device_id=where, device_id_type=MESH
        )

    patches = [video_patches[frame_video[me * 2 + f]] for f in range(2)]

    frames = videos.shape[1]
    at_row = lax.broadcasted_iota(jnp.int32, (frames, frames), 0)
    at_col = lax.broadcasted_iota(jnp.int32, (frames, frames), 1)
    pick = (at_col == 2 * (at_row % GROUPS) + at_row // GROUPS).astype(F32).astype(BF16)
    wide = jnp.broadcast_to(videos[...], (8, frames)).astype(F32).astype(BF16)
    down = lax.dot_general(pick, wide, NT, preferred_element_type=F32)
    along = lax.dot_general(wide, pick, NT, preferred_element_type=F32)
    bias[...] = jnp.where(down[:, :1] == along[:1, :], F32(0.0), F32(-1e30))

    scale = F32(HD**-0.5)
    key_at = lax.broadcasted_iota(jnp.int32, (PMAX, PMAX), 1)

    def build(n):
        for j in range(5):
            load(n, j).wait()
        for f in range(2):
            rows = slice(f * PMAX, (f + 1) * PMAX)
            for j in range(per):
                at = (rows, slice((n * per + j) * HD, (n * per + j + 1) * HD))
                scores = lax.dot_general(qs[at], ks[at], NT, preferred_element_type=F32) * scale
                probs = softmax_rows(jnp.where(key_at < patches[f], scores, F32(-1e30)))
                value = lax.dot_general(probs, vs[at], NN, preferred_element_type=F32)
                spot = f * per + j
                stage[pl.ds(spot, PMAX, stride=height), :] = qt[at].astype(F32)
                stage[pl.ds(2 * per + spot, PMAX, stride=height), :] = kt[at].astype(F32)
                stage[pl.ds(4 * per + spot, PMAX, stride=height), :] = value

        def pack(i, carry):
            block = stage[pl.ds(pl.multiple_of(i * 16 * height, 16), 16 * height), :]
            f_send[n, pl.ds(i * 16, 16)] = block.reshape(16, height, HD).astype(BF16)
            return carry

        lax.fori_loop(0, GROUPS // 16, pack, 0)

    def unpack(src, yy):
        for i in range(plane // 16):
            block = src[pl.ds(yy * plane + i * 16, 16)].astype(F32)
            at = pl.ds(pl.multiple_of((yy * plane + i * 16) * height, 16), 16 * height)
            stage[at, :] = block.reshape(16 * height, HD)

    def exchange(send_buf, recv_buf, sems, first, last):
        def body(i, carry):
            g2, s2 = peer(i)
            remote(send_buf.at[g2 * NZ + s2], recv_buf.at[me], sems.at[0], sems.at[1], {"grp": g2, "sp": s2}).start()
            return carry

        lax.fori_loop(max(first, 1), last, body, 0)

    def exchanged(send_buf, recv_buf, sems, k):
        some = pl.ds(0, plane if k else plane - 1)
        return remote(send_buf.at[some], recv_buf.at[some], sems.at[0], sems.at[1], {"tp": core})

    def send_part(n, b):
        step = GROUPS // 8
        exchange(f_send.at[n], f_recv.at[n], sem_f.at[n, b * step // plane], b * step, (b + 1) * step)

    def z_copy(step, sign):
        zz = (z - sign * step + NZ) % NZ
        lane = 0 if sign > 0 else 1
        return remote(
            wy.at[y, zz], wy.at[y, zz], sem_wz_s.at[lane, step], sem_wz_r.at[lane, step], {"sp": (z + sign + NZ) % NZ}
        )

    z_plan = ((0, 1), (0, -1), (1, 1), (1, -1), (2, 1), (2, -1), (3, 1))

    def z_next(step):
        for sign in (1, -1):
            if (step, sign) in z_plan:
                z_copy(step, sign).wait_recv()
            if (step + 1, sign) in z_plan:
                z_copy(step + 1, sign).start()

    def y_copy(e, d):
        zz = (z - e + NZ) % NZ
        return remote(
            wy.at[y, zz], wy.at[y, zz], sem_wy_s.at[e, d - 1], sem_wy_r.at[e, d - 1],
            {"grp": ((y + d) % NY) * NX + x},
        )

    def t_copy(n, k, d):
        at = (y + k) % NY
        return remote(
            tall.at[n, x, at], tall.at[n, x, at], sem_t_s.at[n, k, d - 1], sem_t_r.at[n, k, d - 1],
            {"grp": y * NX + (x + d) % NX},
        )

    def t_next(n, k, sign):
        at = (y + k) % NY
        rows = pl.ds(0 if sign > 0 else plane, plane)
        piece = tall.at[n, (x - sign + NX) % NX, at, rows]
        lane = 1 if sign > 0 else 3
        return remote(
            piece, piece, sem_t_s.at[n, k, lane], sem_t_r.at[n, k, lane], {"grp": y * NX + (x + sign + NX) % NX}
        )

    def t_pass(n, k):
        for sign in (1, -1):
            t_copy(n, k, sign % NX).wait_recv()
            t_next(n, k, sign).start()

    def t_rest(n):
        if n < parts - LATE:
            return [functools.partial(t_next, n, sign=s) for s in (1, -1)]
        return [functools.partial(t_copy, n, d=d) for d in around]

    def spread(e):
        for d in around:
            y_copy(e, d).start()

    around = (1, 3, 2)

    build(0)
    load_w.wait()
    pl.semaphore_wait(barrier, GROUPS)
    for sign in (1, -1):
        z_copy(0, sign).start()
    plan = {
        2: (0, (0,)),
        4: (1, (1, 7)),
        6: (2, (2, 6)),
        7: (None, (3, 5)),
    }
    for b in range(8):
        send_part(0, b)
        if b in plan:
            step, shards = plan[b]
            if step is not None:
                z_next(step)
            for e in shards:
                spread(e)
    build(1)
    send_part(1, 0)
    z_next(3)
    spread(4)
    for b in range(1, 8):
        send_part(1, b)
    build(2)
    for n in range(parts):
        f_recv[n, me] = f_send[n, me]

    odd = x % 2
    third = NZ * cols
    small = third // 3

    def order_weights():
        for e in range(NZ):
            for d in around:
                y_copy(e, d).wait_recv()
        for yy in range(NY):
            block = wy[yy].astype(F32).reshape(third, heads * HD)
            base = (yy // 2) * 2 * third
            big = jnp.where(odd == 0, block[: 2 * small], block[small:]).astype(BF16)
            wfull[base + (yy % 2) * 2 * small : base + (yy % 2 + 1) * 2 * small, :] = big
            rest = jnp.where(odd == 0, block[2 * small :], block[:small]).astype(BF16)
            spot = odd + (yy % 2) - 2 * odd * (yy % 2)
            wfull[pl.ds(pl.multiple_of(base + 4 * small + spot * small, 16), small), :] = rest

    for n in range(parts):
        if 0 < n <= parts - LATE:
            for k in range(NY):
                t_pass(n - 1, k)
        for k in range(NY):
            exchanged(f_send.at[n], f_recv.at[n], sem_f.at[n, k], k).wait_recv()
            unpack(f_recv.at[n], (y - k + NY) % NY)
        for j in range(per):
            q, k, v = (
                jnp.concatenate(
                    [stage[pl.ds(t * 2 * per + f * per + j, GROUPS, stride=height), :] for f in range(2)], axis=0
                ).astype(BF16)
                for t in range(3)
            )
            scores = lax.dot_general(q, k, NT, preferred_element_type=F32) * scale
            probs = softmax_rows(scores + bias[...])
            value = lax.dot_general(probs, v, NN, preferred_element_type=F32)
            for k in range(NY):
                for f in range(2):
                    rows = value[f * GROUPS + k * plane : f * GROUPS + (k + 1) * plane]
                    tall[n, x, k, f * plane : (f + 1) * plane, j * HD : (j + 1) * HD] = rows.astype(BF16)
        for k in range(NY):
            if n < parts - 1:
                send_part(parts - 1, n * NY + k)
            for d in (1, 3) if n < parts - LATE else around:
                t_copy(n, k, d).start()

    order_weights()

    width = 2 * third
    feats = per * HD

    def product(k, c, groups):
        total = None
        for n in groups:
            left = jnp.concatenate([tall[n, s, (y + k) % NY] for s in range(NX)], axis=0)
            right = wfull[pl.ds(pl.multiple_of(c * width, 16), width), n * feats : (n + 1) * feats]
            term = lax.dot_general(left, right, NT, preferred_element_type=F32)
            total = term if total is None else total + term
        return total

    def part_copy(k):
        return remote(part.at[k], part_recv.at[k], sem_part_s.at[k], sem_part_r.at[k], {"tp": 1 - core})

    for k in range(NY):
        for n in range(parts - 1):
            for c in t_rest(n):
                c(k=k).wait_recv()
        part[k] = product(k, 1 - core, range(parts - 1))
        own[k] = product(k, core, range(parts - 1))

    for k in range(NY):
        if not LATE:
            for i in ((0, 1), (2,), (3,), ())[k]:
                t_pass(parts - 1, i)
        for c in t_rest(parts - 1):
            c(k=k).wait_recv()
        part[k] += product(k, 1 - core, (parts - 1,))
        part_copy(k).start()
        own[k] += product(k, core, (parts - 1,))
        part_copy(k).wait_recv()
        total = own[k] + part_recv[k]
        for s in range(NX):
            for f in range(2):
                for j in range(width // HD):
                    stage[pl.ds((s * 2 + f) * (width // HD) + j, plane, stride=height), :] = total[
                        (s * 2 + f) * plane : (s * 2 + f + 1) * plane, j * HD : (j + 1) * HD
                    ]
        for i in range(plane // 16):
            block = stage[i * 16 * height : (i + 1) * 16 * height, :]
            o_send[pl.ds(((y + k) % NY) * plane + i * 16, 16)] = block.reshape(16, height, HD).astype(BF16)
        exchange(o_send, o_recv, sem_o.at[k], k * plane, (k + 1) * plane)
        if k == 0:
            o_recv[me] = o_send[me]

    for n in range(parts):
        for k in range(NY):
            exchanged(f_send.at[n], f_recv.at[n], sem_f.at[n, k], k).wait_send()
            for d in (1, 3) if n < parts - LATE else around:
                t_copy(n, k, d).wait_send()
            if n < parts - LATE:
                for sign in (1, -1):
                    t_next(n, k, sign).wait_send()
    for k in range(NY):
        part_copy(k).wait_send()
    for step, sign in z_plan:
        z_copy(step, sign).wait_send()
    for e in range(NZ):
        for d in around:
            y_copy(e, d).wait_send()

    row_at = lax.broadcasted_iota(jnp.int32, (plane, HD), 0)
    low = lax.broadcasted_iota(jnp.int32, (plane, HD), 1) < HD // 2

    def store(yy, f, k):
        rows = pl.ds(pl.multiple_of(f * PMAX + yy * plane, plane), plane)
        return pltpu.make_async_copy(out.at[rows], out_hbm.at[rows], sem_out.at[k, f])

    def finish(yy):
        for f in range(2):
            alive = row_at + yy * plane < patches[f]

            def piece(xx, j):
                return jnp.concatenate(
                    [stage[pl.ds(((yy * NX + xx) * NZ) * height + (s * 2 + f) * (width // HD) + j, NZ, stride=height), :]
                     for s in range(NX)], axis=0)

            def put(at, value):
                rows = pl.ds(pl.multiple_of(f * PMAX + yy * plane, plane), plane)
                out[rows, at * HD : (at + 1) * HD] = jnp.where(alive, value, F32(0.0)).astype(BF16)

            for m in range(NX // 2):
                left, right = piece(2 * m, 2), piece(2 * m + 1, 2)
                middle = (
                    jnp.where(low, left, right),
                    pltpu.roll(jnp.where(low, right, left), HD // 2, 1),
                )
                for half in range(2):
                    at = half * (NX * third // HD) + m * (2 * third // HD)
                    put(at, piece(2 * m, half))
                    put(at + 1, middle[half])
                    put(at + 2, piece(2 * m + 1, half))

    for k in range(NY):
        yy = (y - k + NY) % NY
        exchanged(o_send, o_recv, sem_o.at[k], k).wait_recv()
        unpack(o_recv, yy)
        finish(yy)
        for f in range(2):
            store(yy, f, k).start()
    for k in range(NY):
        exchanged(o_send, o_recv, sem_o.at[k], k).wait_send()
        for f in range(2):
            store((y - k + NY) % NY, f, k).wait()


def per_device(q_spatial, k_spatial, v_spatial, q_temporal, k_temporal, out_weight, frame_video, video_patches):
    rows, feats = q_spatial.shape
    heads = feats // HD
    cols = out_weight.shape[1]
    frames = rows // PMAX
    anywhere = pl.BlockSpec(memory_space=pl.ANY)
    scalars = pl.BlockSpec(memory_space=pltpu.SMEM)
    parts = PARTS
    height = 3 * frames * heads // parts
    all_frames = frame_video.shape[0]
    width = 2 * NZ * cols
    dma = pltpu.SemaphoreType.DMA
    return pl.pallas_call(
        functools.partial(kernel, heads, parts),
        out_shape=jax.ShapeDtypeStruct((rows, feats), BF16),
        in_specs=[anywhere] * 6 + [pl.BlockSpec(memory_space=pltpu.VMEM), scalars, scalars],
        out_specs=anywhere,
        scratch_shapes=[pltpu.VMEM((rows, feats), BF16)] * 6 + [
            pltpu.VMEM((all_frames, all_frames), F32),
            pltpu.VMEM((GROUPS * height, HD), F32),
            pltpu.VMEM((parts, GROUPS, height, HD), BF16),
            pltpu.VMEM((parts, GROUPS, height, HD), BF16),
            pltpu.VMEM((GROUPS, height, HD), BF16),
            pltpu.VMEM((GROUPS, height, HD), BF16),
            pltpu.VMEM((parts, NX, NY, all_frames // NY, feats // parts), BF16),
            pltpu.VMEM((NY, NZ, cols, feats), BF16),
            pltpu.VMEM((2 * width, feats), BF16),
            pltpu.VMEM((NY, all_frames, width), F32),
            pltpu.VMEM((NY, all_frames, width), F32),
            pltpu.VMEM((NY, all_frames, width), F32),
            dma((parts + 1, 5)),
            dma((NY, 2)),
            dma((parts, NY, 2)),
            dma((NY, 2)),
            dma((parts, NY, 4)),
            dma((parts, NY, 4)),
            dma((NY,)),
            dma((NY,)),
            dma((2, 4)),
            dma((2, 4)),
            dma((NZ, 3)),
            dma((NZ, 3)),
        ],
        compiler_params=pltpu.CompilerParams(
            collective_id=0, has_side_effects=True, vmem_limit_bytes=58 * 2**20
        ),
    )(
        q_spatial, k_spatial, v_spatial, q_temporal, k_temporal, out_weight.T,
        frame_video[None, :], frame_video, video_patches,
    )


def solution(mesh):
    return jax.shard_map(
        per_device,
        mesh=mesh,
        in_specs=(
            P(("grp", "sp"), "tp"),
            P(("grp", "sp"), "tp"),
            P(("grp", "sp"), "tp"),
            P(("grp", "sp"), "tp"),
            P(("grp", "sp"), "tp"),
            P("tp", ("grp", "sp")),
            P(),
            P(),
        ),
        out_specs=P(("grp", "sp"), "tp"),
        check_vma=False,
    )
```

time: 127 us -> 116 us (0.913)
  Pallas kernels: 121 us -> 114 us
  local copies, waits for them, and re-layouts: 5.9 us -> 2.06 us
    pallas_call x1, Pallas kernels: 121 us -> 114 us  [per_device(): pl.pallas_call(functools.partial(kernel, heads, parts), out_shape=jax.Sha...]
    unnamed x10 -> x1, local copies, waits for them, and re-layouts: 4.84 us -> 2.06 us
where the time goes in v3:
time: 116 us
  Pallas kernels  114 us (98%)
  local copies, waits for them, and re-layouts  2.06 us (2%)
    pallas_call x1, Pallas kernels, per_device(): pl.pallas_call(functools.partial(kernel, heads, parts), out_shape=jax.Sha...  114 us

profile of v3, /device:TPU:1, one launch (start us, length us, event | category | flops | bytes accessed | tf_op | source)
XLA Modules:
  0.0 116.0 jit_solution(3743043985584450108)
XLA Ops:
  0.0 113.9 %shard_map.82 = bf16[256,1536]{1,0:T(8,128)(2,1)} custom-call(bf16[256,1536]{1,0:T(8,128)(2,1)} %qs_hbm.1, bf16[256,1536]{1,0:T(8,128)(2,1)} %ks_hbm.1, bf16[256,1536]{1,0:T(8,128)(2,1)} %vs_hbm.1, bf16[256,1536]{1,0:T(8,128)(2,1)} %qt_hbm.1, bf16[256,1536]{1,0:T(8,128)(2,1)} %kt_hbm.1, bf16[24,1536]{1,0:T(8,128)(2,1)} %bitcast.2, s32[1,256]{1,0:T(1,128)} %bitcast.3, ...), custom_call_target="tpu_custom_call" | custom-call | tf_op jit(solution)/shard_map/pallas_call | solution.py:384
  113.9 2.1 %copy.10 = bf16[256,1536]{1,0:T(8,128)(2,1)} copy(bf16[256,1536]{1,0:T(8,128)(2,1)} %shard_map.82) | data formatting | bytes 1572864

commit v4 on v3

--- a/solution.py
+++ b/solution.py
@@ -117,8 +117,8 @@
             stage[at, :] = block.reshape(16 * height, HD)
 
     def exchange(send_buf, recv_buf, sems, first, last):
-        def body(i, carry):
-            g2, s2 = peer(i)
+        def body(j, carry):
+            g2, s2 = peer(first + ((j - first) * 13) % plane)
             remote(send_buf.at[g2 * NZ + s2], recv_buf.at[me], sems.at[0], sems.at[1], {"grp": g2, "sp": s2}).start()
             return carry
 
@@ -130,7 +130,17 @@
 
     def send_part(n, b):
         step = GROUPS // 8
-        exchange(f_send.at[n], f_recv.at[n], sem_f.at[n, b * step // plane], b * step, (b + 1) * step)
+
+        def body(j, carry):
+            i = (j * 37) % GROUPS
+            g2, s2 = peer(i)
+            remote(
+                f_send.at[n, g2 * NZ + s2], f_recv.at[n, me], sem_f.at[n, i // plane, 0], sem_f.at[n, i // plane, 1],
+                {"grp": g2, "sp": s2},
+            ).start()
+            return carry
+
+        lax.fori_loop(max(b * step, 1), (b + 1) * step, body, 0)
 
     def z_copy(step, sign):
         zz = (z - sign * step + NZ) % NZ

time: 116 us -> 114 us (0.983)
  Pallas kernels: 114 us -> 112 us
    pallas_call x1, Pallas kernels: 114 us -> 112 us  [per_device(): pl.pallas_call(functools.partial(kernel, heads, parts), out_shape=jax.Sha...]
where the time goes in v4:
time: 114 us
  Pallas kernels  112 us (98%)
  local copies, waits for them, and re-layouts  2.06 us (2%)
    pallas_call x1, Pallas kernels, per_device(): pl.pallas_call(functools.partial(kernel, heads, parts), out_shape=jax.Sha...  112 us

profile of v4, /device:TPU:1, one launch (start us, length us, event | category | flops | bytes accessed | tf_op | source)
XLA Modules:
  0.0 114.0 jit_solution(3449290284553138434)
XLA Ops:
  0.0 112.0 %shard_map.82 = bf16[256,1536]{1,0:T(8,128)(2,1)} custom-call(bf16[256,1536]{1,0:T(8,128)(2,1)} %qs_hbm.1, bf16[256,1536]{1,0:T(8,128)(2,1)} %ks_hbm.1, bf16[256,1536]{1,0:T(8,128)(2,1)} %vs_hbm.1, bf16[256,1536]{1,0:T(8,128)(2,1)} %qt_hbm.1, bf16[256,1536]{1,0:T(8,128)(2,1)} %kt_hbm.1, bf16[24,1536]{1,0:T(8,128)(2,1)} %bitcast.2, s32[1,256]{1,0:T(1,128)} %bitcast.3, ...), custom_call_target="tpu_custom_call" | custom-call | tf_op jit(solution)/shard_map/pallas_call | solution.py:394
  112.0 2.1 %copy.10 = bf16[256,1536]{1,0:T(8,128)(2,1)} copy(bf16[256,1536]{1,0:T(8,128)(2,1)} %shard_map.82) | data formatting | bytes 1572864
